TPU v7x, 512 devices: a whole 4x4x16 slice. The times are simulated.
512 devices in a mesh: ctx: 64 (over y_hi, z, core), tp: 8 (over y_lo, x).
Axes of the slice: x: 4, y: 4 (y_hi: 2, y_lo: 2; y = y_hi * 2 + y_lo), z: 16, core: 2. Of those that a mesh axis runs over, the one named last changes fastest.
Arguments:
- context_query: bfloat16 [65536, 32, 128], P('ctx', 'tp'), may hold values from -140 to 140
- context_pairs: bfloat16 [65536, 8, 2, 128], P('ctx', 'tp'), may hold values from -6 to 6
- anchor_block: int32 [1], replicated, may hold values from 0 to 63
- answer_query: bfloat16 [64, 32, 128], P('ctx', 'tp'), may hold values from -256 to 256
- answer_pairs: bfloat16 [64, 8, 2, 128], P('ctx', 'tp'), may hold values from -6 to 6
- output_weight: bfloat16 [4096, 8192], P('tp', 'ctx'), may hold values from -0.09375 to 0.09375
Outputs:
- context_heads: bfloat16 [65536, 32, 128], P('ctx', 'tp')
- answer_output: bfloat16 [64, 8192], P('tp', 'ctx')
All inputs are finite; a program needn't handle non-finite values.
Results may differ from a plain program's by a relative error of at most 0.019.
Values may be sent and summed in bfloat16 or wider, within the bound.
A program may use at most 64 MiB of HBM per device.

v0:
```python
import jax
import jax.numpy as jnp
from jax import lax
from jax.sharding import PartitionSpec as P


def from_root(block, axis, owner):
    block = jnp.where(lax.axis_index(axis) == owner, block, jnp.zeros_like(block))
    return lax.psum(block, axis)


def merged_2(value, axis, join):
    pieces = jax.tree.map(lambda part: lax.all_gather(part, axis), value)
    head = jax.tree.map(lambda part: part[0], pieces)
    tail = jax.tree.map(lambda part: part[1:], pieces)
    running, _ = lax.scan(lambda running, share: (join(running, share), None), head, tail)
    return running


def combine_parts(first, second):
    peak = jnp.maximum(first[0], second[0])
    first_rescale = jnp.exp(first[0] - peak)
    second_rescale = jnp.exp(second[0] - peak)
    weight_sum = first[1] * first_rescale + second[1] * second_rescale
    numerator = first[2] * first_rescale[..., None] + second[2] * second_rescale[..., None]
    return (peak, weight_sum, numerator)


def self_part(rows_query, self_pairs):
    score_scale = rows_query.shape[-1] ** (-0.5)
    scores = (
        jnp.einsum(
            "qhd,sd->hqs", rows_query, self_pairs[:, 0, :], preferred_element_type=jnp.float32
        )
        * score_scale
    )
    row_positions = jnp.arange(rows_query.shape[0])
    causal = jnp.arange(self_pairs.shape[0])[None, :] <= row_positions[:, None]
    scores = jnp.where(causal[None], scores, -jnp.inf)
    peak = jnp.max(scores, axis=-1)
    probs = jnp.exp(scores - peak[..., None])
    weight_sum = jnp.sum(probs, axis=-1)
    numerator = jnp.einsum(
        "hqs,sd->hqd",
        probs.astype(jnp.bfloat16),
        self_pairs[:, 1, :],
        preferred_element_type=jnp.float32,
    )
    return (peak, weight_sum, numerator)


def on_device(
    context_query, context_pairs, anchor_block, answer_query, answer_pairs, output_weight
):
    block_index = lax.axis_index("ctx")
    anchor_index = anchor_block[0]
    anchor_pairs = from_root(context_pairs, "ctx", anchor_index)
    is_anchor = block_index == anchor_index
    own_keys = context_pairs[:, 0, 0, :]
    own_values = context_pairs[:, 0, 1, :]
    far_keys = anchor_pairs[:, 0, 0, :]
    far_values = anchor_pairs[:, 0, 1, :]
    block_length = context_query.shape[0]
    score_scale = context_query.shape[-1] ** (-0.5)
    positions = jnp.arange(block_length)
    causal = positions[None, :] <= positions[:, None]

    def one_head(head_query):
        own_scores = (
            jnp.einsum("td,sd->ts", head_query, own_keys, preferred_element_type=jnp.float32)
            * score_scale
        )
        far_scores = (
            jnp.einsum("td,sd->ts", head_query, far_keys, preferred_element_type=jnp.float32)
            * score_scale
        )
        own_scores = jnp.where(causal, own_scores, -jnp.inf)
        far_scores = jnp.where(is_anchor, -jnp.inf, far_scores)
        peak = jnp.maximum(jnp.max(own_scores, axis=-1), jnp.max(far_scores, axis=-1))
        own_probs = jnp.exp(own_scores - peak[:, None])
        far_probs = jnp.exp(far_scores - peak[:, None])
        weight_sum = jnp.sum(own_probs, axis=-1) + jnp.sum(far_probs, axis=-1)
        mixed = jnp.dot(
            own_probs.astype(jnp.bfloat16), own_values, preferred_element_type=jnp.float32
        )
        mixed = mixed + jnp.dot(
            far_probs.astype(jnp.bfloat16), far_values, preferred_element_type=jnp.float32
        )
        return (mixed / weight_sum[:, None]).astype(jnp.bfloat16)

    head_outputs = lax.map(one_head, jnp.transpose(context_query, (1, 0, 2)))
    context_heads = jnp.transpose(head_outputs, (1, 0, 2))
    all_query, all_pairs = (
        lax.all_gather(answer_query, "ctx", axis=0, tiled=True),
        lax.all_gather(answer_pairs, "ctx", axis=0, tiled=True),
    )
    self_pairs = all_pairs[:, 0, :, :]
    far_scores = (
        jnp.einsum("qhd,sd->hqs", all_query, own_keys, preferred_element_type=jnp.float32)
        * score_scale
    )
    peak = jnp.max(far_scores, axis=-1)
    far_probs = jnp.exp(far_scores - peak[..., None])
    weight_sum = jnp.sum(far_probs, axis=-1)
    numerator = jnp.einsum(
        "hqs,sd->hqd",
        far_probs.astype(jnp.bfloat16),
        own_values,
        preferred_element_type=jnp.float32,
    )
    answer_count = all_query.shape[0]
    merged = merged_2((peak, weight_sum, numerator), "ctx", combine_parts)
    finished = combine_parts(merged, self_part(all_query, self_pairs))
    answer_heads = (finished[2] / finished[1][..., None]).astype(jnp.bfloat16)
    answer_flat = jnp.transpose(answer_heads, (1, 0, 2)).reshape(answer_count, -1)
    answer_output = lax.psum_scatter(
        jnp.dot(answer_flat, output_weight, preferred_element_type=jnp.float32).astype(
            jnp.bfloat16
        ),
        "tp",
        scatter_dimension=0,
        tiled=True,
    )
    return (context_heads, answer_output)


def solution(mesh):
    in_specs = (
        P("ctx", "tp", None),
        P("ctx", "tp", None, None),
        P(),
        P("ctx", "tp", None),
        P("ctx", "tp", None, None),
        P("tp", "ctx"),
    )
    out_specs = (P("ctx", "tp", None), P("tp", "ctx"))
    return jax.shard_map(
        on_device, mesh=mesh, in_specs=in_specs, out_specs=out_specs, check_vma=False
    )
```

profile of v0, /device:TPU:1, one launch (start us, length us, event | category | flops | bytes accessed | tf_op | source)
XLA Modules:
  0.0 809.6 jit_solution(8528687783850819504)
XLA Ops:
  7.9 1.9 broadcast_select_fusion
  9.9 85.0 %all_gather.24 = bf16[64,4,128]{2,1,0:T(4,128)(2,1)S(1)} all-gather(bf16[1,4,128]{2,1,0:T(4,128)(2,1)} %param.13), channel_id=1, replica_groups=mesh['ctx'=64,'tp'=8] {'ctx'}, dimensions={0}, use_global_device_ids=true | all-gather | bytes 66560 | tf_op jit(solution)/shard_map/all_gather | solution.py:94
  96.4 1.4 copy.55
  97.8 71.9 %all-gather.3 = f32[64,4,64]{2,1,0:T(4,128)S(1)} all-gather(f32[1,4,64]{2,1,0:T(4,128)S(1)} %bitcast.115), channel_id=2, replica_groups=mesh['ctx'=64,'tp'=8] {'ctx'}, dimensions={0}, use_global_device_ids=true | all-gather | bytes 66560 | tf_op jit(solution)/shard_map/all_gather | solution.py:13
  170.0 73.3 %all-gather.4 = f32[64,4,64]{2,1,0:T(4,128)S(1)} all-gather(f32[1,4,64]{2,1,0:T(4,128)S(1)} %bitcast.116), channel_id=3, replica_groups=mesh['ctx'=64,'tp'=8] {'ctx'}, dimensions={0}, use_global_device_ids=true | all-gather | bytes 66560 | tf_op jit(solution)/shard_map/all_gather | solution.py:13
  243.3 71.1 %all_gather.31 = bf16[64,1,2,128]{3,2,1,0:T(2,128)(2,1)S(1)} all-gather(bf16[1,1,2,128]{3,2,1,0:T(2,128)(2,1)S(1)} %copy-done.3), channel_id=1, replica_groups=mesh['ctx'=64,'tp'=8] {'ctx'}, dimensions={0}, use_global_device_ids=true | all-gather | bytes 33280 | tf_op jit(solution)/shard_map/all_gather | solution.py:95
  314.5 1.3 dynamic-slice
  316.7 217.6 %all-reduce.3.cloned.1.call-done = bf16[1024,1,2,128]{3,0,2,1:T(8,128)(2,1)} async-done(((bf16[1024,1,2,128]{3,0,2,1:T(8,128)(2,1)}), bf16[1024,1,2,128]{3,0,2,1:T(8,128)(2,1)}) %all-reduce.3.cloned.1.call-update) | async-done | bytes 524304 | tf_op jit(solution)/shard_map/psum | solution.py:9
  535.4 21.4 %while.26 = (s32[]{:T(128)}, bf16[4,1024,128]{2,1,0:T(8,128)(2,1)}, bf16[4,1024,128]{2,1,0:T(8,128)(2,1)S(1)}, bf16[1024,128]{1,0:T(8,128)(2,1)S(1)}, pred[]{:T(...) while((s32[]{:T(128)}, bf16[4,1024,128]{2,1,0:T(8,128)(2,1)}, ...), condition=%wide.region_6.7_spmd.clone, body=%wide.region_1.6_spmd.clone.sunk | while | flops 1100347392 | bytes 28106868 | solution.py:91
  537.8 1.3 fusion.103
  539.2 1.6 fusion.104
  543.2 1.3 fusion.103
  544.5 1.5 fusion.104
  548.5 1.3 fusion.103
  549.8 1.6 fusion.104
  553.8 1.3 fusion.103
  555.2 1.6 fusion.104
  556.7 3.0 copy.54
  559.7 137.3 %all-gather.7.cloned.1.call-done = f32[256,64,128]{2,1,0:T(8,128)} async-done(((f32[4,64,128]{2,1,0:T(8,128)}), f32[256,64,128]{2,1,0:T(8,128)}) %all-gather.7.cloned.1.call-update) | async-done | bytes 8388624 | tf_op jit(solution)/shard_map/all_gather | solution.py:13
  697.0 8.2 %slice.67 = f32[252,64,128]{2,1,0:T(8,128)} slice(f32[256,64,128]{2,1,0:T(8,128)} %all-gather.7.cloned.1.call-done), slice={[4:256], [0:64], [0:128]} | slice | bytes 16515072 | tf_op jit(solution)/shard_map/slice | solution.py:15
  705.3 70.3 %while.25 = (s32[]{:T(128)}, f32[4,64]{1,0:T(4,128)S(1)}, f32[4,64]{1,0:T(4,128)S(1)}, f32[4,64,128]{2,1,0:T(8,128)S(1)}, f32[63,4,64]{2,1,0:T(4,128)S(1)}, /*in...) while((s32[]{:T(128)}, f32[4,64]{1,0:T(4,128)S(1)}, f32[4,64]{1,0:T(4,128)S(1)}, ...), condition=%wide.region_10.11_spmd, body=%wide.region_9.10_spmd.sunk | while | flops 99842 | bytes 403557 | solution.py:16
  706.4 1.1 fusion.93
  708.6 1.1 fusion.93
  710.9 1.1 fusion.93
  713.1 1.1 fusion.93
  715.3 1.1 fusion.93
  717.6 1.1 fusion.93
  719.8 1.1 fusion.93
  720.9 1.1 fusion.93
  722.0 1.1 fusion.93
  723.1 1.1 fusion.93
  724.3 1.1 fusion.93
  725.4 1.1 fusion.93
  727.6 1.1 fusion.93
  729.8 1.1 fusion.93
  732.1 1.1 fusion.93
  734.3 1.1 fusion.93
  736.5 1.1 fusion.93
  738.8 1.1 fusion.93
  741.0 1.1 fusion.93
  742.1 1.1 fusion.93
  743.2 1.1 fusion.93
  744.3 1.1 fusion.93
  745.5 1.1 fusion.93
  746.6 1.1 fusion.93
  748.8 1.1 fusion.93
  751.0 1.1 fusion.93
  776.0 26.2 %all-reduce = bf16[64,128]{1,0:T(8,128)(2,1)S(1)} all-reduce(bf16[64,128]{1,0:T(8,128)(2,1)S(1)} %convolution_convert_fusion), channel_id=5, replica_groups=mesh['ctx'=64,'tp'=8] {'tp'}, use_global_device_ids=true, to_apply=%region_13.14.clone | all-reduce | flops 8192 | bytes 32768
  (154 shorter events, 55.1 us)
Async XLA Ops:
  7.2 768.6 %copy-start = (bf16[512,128]{1,0:T(8,128)(2,1)S(1)}, bf16[512,128]{1,0:T(8,128)(2,1)}, u32[]{:S(2)}) copy-start(bf16[512,128]{1,0:T(8,128)(2,1)} %param.15) | copy-start | bytes 393220
  7.2 527.1 %all-reduce.3.cloned.1.call-start = ((), (), s32[]{:S(2)}) async-start(), calls=%async_computation | async-start | bytes 1048576 | tf_op jit(solution)/shard_map/psum | solution.py:9
  7.9 235.4 %copy-start.3 = (bf16[1,1,2,128]{3,2,1,0:T(2,128)(2,1)S(1)}, bf16[1,1,2,128]{3,2,1,0:T(2,128)(2,1)}, u32[]{:S(2)}) copy-start(bf16[1,1,2,128]{3,2,1,0:T(2,128)(2,1)} %param.14) | copy-start | bytes 1540
  9.9 687.2 %all-gather.7.cloned.1.call-start = ((), (), s32[]{:S(2)}) async-start(), calls=%async_computation.1 | async-start | bytes 8519680 | tf_op jit(solution)/shard_map/all_gather | solution.py:13
  169.7 365.7 %copy-start.1 = (f32[64,4,64]{2,1,0:T(4,128)}, f32[64,4,64]{2,1,0:T(4,128)S(1)}, u32[]{:S(2)}) copy-start(f32[64,4,64]{2,1,0:T(4,128)S(1)} %all-gather.3) | copy-start | bytes 196612
  243.3 292.1 %copy-start.2 = (f32[64,4,64]{2,1,0:T(4,128)}, f32[64,4,64]{2,1,0:T(4,128)S(1)}, u32[]{:S(2)}) copy-start(f32[64,4,64]{2,1,0:T(4,128)S(1)} %all-gather.4) | copy-start | bytes 196612
  697.0 8.2 %slice-start = ((f32[256,64,128]{2,1,0:T(8,128)}), f32[4,64,128]{2,1,0:T(8,128)S(1)}, s32[]{:S(2)}) async-start(f32[256,64,128]{2,1,0:T(8,128)} %all-gather.7.cloned.1.call-done), calls=%async_computation.2 | async-start | bytes 262144 | tf_op jit(solution)/shard_map/slice | solution.py:14
  697.0 8.2 %slice-start.1 = ((f32[64,4,64]{2,1,0:T(4,128)}), f32[63,4,64]{2,1,0:T(4,128)S(1)}, s32[]{:S(2)}) async-start(f32[64,4,64]{2,1,0:T(4,128)} %copy-done.1), calls=%async_computation.3 | async-start | bytes 258048 | tf_op jit(solution)/shard_map/slice | solution.py:15
  697.0 8.2 %slice-start.2 = ((f32[64,4,64]{2,1,0:T(4,128)}), f32[63,4,64]{2,1,0:T(4,128)S(1)}, s32[]{:S(2)}) async-start(f32[64,4,64]{2,1,0:T(4,128)} %copy-done.2), calls=%async_computation.4 | async-start | bytes 258048 | tf_op jit(solution)/shard_map/slice | solution.py:15
Sparse Core Ops, SparseCore 0:
  11.5 522.7 all-reduce.2
  538.1 158.8 all-gather.6
where the time goes:
time: 817 us; the launch traced here: 810 us
  waiting for transfers between devices  355 us (43%)
  blocking collectives  328 us (40%)
  other arithmetic  76.7 us (9%)
  matrix products  17.8 us (2%)
  local copies, waits for them, and re-layouts  15.6 us (2%)
  between operations  15.5 us (2%)
    psum x1, waiting for transfers between devices, from_root(): return lax.psum(block, axis)  218 us
    all_gather x2, blocking collectives, merged_2(): pieces = jax.tree.map(lambda part: lax.all_gather(part, axis), value)  145 us
    all_gather x1, waiting for transfers between devices, merged_2(): pieces = jax.tree.map(lambda part: lax.all_gather(part, axis), value)  137 us
    all_gather x1, blocking collectives, on_device(): lax.all_gather(answer_query, 'ctx', axis=0, tiled=True)  85 us
    all_gather x1, blocking collectives, on_device(): lax.all_gather(answer_pairs, 'ctx', axis=0, tiled=True)  71.1 us
    add x63, other arithmetic, combine_parts(): first[2] * first_rescale[..., None] + second[2] * second_rescale[..., None]  67.5 us
    unnamed x1, blocking collectives  26.2 us
  transfers between devices with their start and end apart: 2, of which 2 were waited for; matrix products, arithmetic and copies ran while one was open for 4% of the time, Pallas kernels for 0%

commit v1 on v0

v1 whole, which is shorter than its diff:
```python
import functools
import math

import jax
import jax.numpy as jnp
from jax import lax
from jax.experimental import pallas as pl
from jax.experimental.pallas import tpu as pltpu
from jax.sharding import PartitionSpec as P

MESH = pl.DeviceIdType.MESH
N_CTX, N_TP, N_Z = 64, 8, 16
HD, GROUP, BLOCK, QTOK = 128, 4, 1024, 64
ROWS = BLOCK * GROUP
SUB = 256
F32, BF16 = jnp.float32, jnp.bfloat16
C2 = HD**-0.5 * math.log2(math.e)


def dot_t(a, b):
    return lax.dot_general(a, b, (((1,), (1,)), ((), ())), preferred_element_type=F32)


def kernel(
    anchor_ref, q_hbm, pairs_hbm, aq_hbm, ap_hbm, w_hbm,
    out_hbm, ans_ref,
    q_v, pairs_v, pairs_f, aq_ref, ap_ref, w_v, out_v,
    kv_own, k_cand, v_cand, z_src, kz_cand, vz_cand, far,
    m_s, l_s, acc_s,
    q_all, akv, o_f, o_src, l_src, o_recv, l_recv, h_src, h_all, p_src, p_recv,
    load_sem, store_sem, send_sem, recv_sem,
):
    c = lax.axis_index("ctx")
    p = lax.axis_index("tp")
    y, z, k = c // 32, (c // 2) % N_Z, c % 2
    rank = 2 * y + k

    def ctx_at(y, z, k):
        return (y * N_Z + z) * 2 + k

    anchor = anchor_ref[0]
    a_rank, a_z = 2 * (anchor // 32) + anchor % 2, (anchor // 2) % N_Z
    is_anchor = anchor == c

    loads = [
        pltpu.make_async_copy(pairs_hbm, pairs_v, load_sem.at[0]),
        pltpu.make_async_copy(q_hbm, q_v, load_sem.at[1]),
        pltpu.make_async_copy(w_hbm, w_v, load_sem.at[2]),
        pltpu.make_async_copy(aq_hbm, aq_ref, load_sem.at[3]),
        pltpu.make_async_copy(ap_hbm, ap_ref, load_sem.at[4]),
    ]
    for load in loads:
        load.start()
    barrier = pltpu.get_barrier_semaphore()
    for d in range(1, N_CTX):
        pl.semaphore_signal(barrier, inc=1, device_id={"ctx": (c + d) % N_CTX}, device_id_type=MESH)
    for d in range(1, N_TP):
        pl.semaphore_signal(barrier, inc=1, device_id={"tp": (p + d) % N_TP}, device_id_type=MESH)

    loads[0].wait()
    pairs_f[...] = pairs_v[...].astype(F32)
    for kv in range(2):
        kv_own[kv] = pairs_f[pl.ds(kv, BLOCK, stride=2), :].astype(BF16).reshape(4, N_Z, 16, HD)
    loads[3].wait()
    loads[4].wait()
    q_all[c] = aq_ref[0]
    pl.semaphore_wait(barrier, N_CTX - 1 + N_TP - 1)

    def send(src, dst, sem, **device):
        pltpu.make_async_remote_copy(
            src_ref=src, dst_ref=dst, send_sem=send_sem.at[sem], recv_sem=recv_sem.at[sem],
            device_id=device, device_id_type=MESH,
        ).start()

    def arrived(ref, sem):
        pltpu.make_async_copy(ref, ref, recv_sem.at[sem]).wait()

    def sent(ref, sem):
        pltpu.make_async_copy(ref, ref, send_sem.at[sem]).wait()

    near = [(y, 1 - k), (1 - y, k), (1 - y, 1 - k)]
    near_cand, z_cand = (k_cand, v_cand), (kz_cand, vz_cand)

    def near_scatter(kv):
        for to_y, to_k in near:
            to = 2 * to_y + to_k
            send(kv_own.at[kv, to], near_cand[kv].at[rank], kv, ctx=ctx_at(to_y, z, to_k))
        near_cand[kv][rank] = kv_own[kv, rank]

    def z_scatter(kv):
        arrived(near_cand[kv].at[pl.ds(0, 3)], kv)
        z_src[kv] = near_cand[kv][a_rank]
        for d in range(1, N_Z):
            to = (z + d) % N_Z
            send(z_src.at[kv, to], z_cand[kv].at[z], 2 + kv, ctx=ctx_at(y, to, k))
        z_cand[kv][z] = z_src[kv, z]

    def z_gather(kv):
        arrived(z_cand[kv].at[pl.ds(0, N_Z - 1)], 2 + kv)
        far[kv, rank, z] = z_cand[kv][a_z]
        for d in range(1, N_Z):
            to = (z + d) % N_Z
            send(far.at[kv, rank, z], far.at[kv, rank, z], 4 + kv, ctx=ctx_at(y, to, k))

    def near_gather(kv):
        arrived(far.at[kv, 0, pl.ds(0, N_Z - 1)], 4 + kv)
        for to_y, to_k in near:
            send(far.at[kv, rank], far.at[kv, rank], 6 + kv, ctx=ctx_at(to_y, z, to_k))

    def far_here(kv):
        arrived(far.at[kv, pl.ds(0, 3)], 6 + kv)

    def own_part(i):
        keys = kv_own[0, 0 : i + 1].reshape((i + 1) * 256, HD)
        values = kv_own[1, 0 : i + 1].reshape((i + 1) * 256, HD)

        def step(j, _):
            rows = pl.ds(pl.multiple_of(i * 1024 + j * SUB, SUB), SUB)
            scores = dot_t(q_v[rows, :], keys)
            token = lax.broadcasted_iota(jnp.int32, (SUB, 256), 0) // GROUP + j * (SUB // GROUP)
            seen = lax.broadcasted_iota(jnp.int32, (SUB, 256), 1) <= token
            last = jnp.where(seen, scores[:, i * 256 :], -jnp.inf)
            scores = jnp.concatenate([scores[:, : i * 256], last], axis=1) if i else last
            peak = jnp.max(scores, axis=1, keepdims=True)
            probs = jnp.exp2((scores - peak) * C2)
            m_s[rows, :] = peak
            l_s[rows, :] = jnp.sum(probs, axis=1, keepdims=True)
            acc_s[rows, :] = jnp.dot(probs.astype(BF16), values, preferred_element_type=F32)
            return 0

        lax.fori_loop(0, 1024 // SUB, step, 0)

    def far_part():
        keys = far[0].reshape(BLOCK, HD)
        values = far[1].reshape(BLOCK, HD)
        far_weight = jnp.where(is_anchor, 0.0, 1.0).astype(F32)

        def step(j, _):
            rows = pl.ds(pl.multiple_of(j * SUB, SUB), SUB)
            scores = dot_t(q_v[rows, :], keys)
            own_peak = m_s[rows, :]
            peak = jnp.maximum(own_peak, jnp.max(scores, axis=1, keepdims=True))
            probs = jnp.exp2((scores - peak) * C2)
            rescale = jnp.where(is_anchor, 1.0, jnp.exp2((own_peak - peak) * C2))
            weight_sum = l_s[rows, :] * rescale + far_weight * jnp.sum(probs, axis=1, keepdims=True)
            mixed = acc_s[rows, :] * rescale + far_weight * jnp.dot(
                probs.astype(BF16), values, preferred_element_type=F32
            )
            out_v[rows, :] = (mixed / weight_sum).astype(BF16)
            return 0

        lax.fori_loop(0, ROWS // SUB, step, 0)

    def answer_part():
        arrived(q_all.at[pl.ds(0, N_CTX - 1)], 8)
        o_f[...] = q_all[...].astype(F32)
        queries = jnp.concatenate([o_f[:, h, :] for h in range(GROUP)], axis=0).astype(BF16)
        scores = dot_t(queries, kv_own[0].reshape(BLOCK, HD))
        peak = jnp.max(scores, axis=1, keepdims=True)
        probs = jnp.exp2((scores - peak) * C2)
        weight_sum = jnp.sum(probs, axis=1, keepdims=True)
        mixed = jnp.dot(
            probs.astype(BF16), kv_own[1].reshape(BLOCK, HD), preferred_element_type=F32
        )
        return queries, peak, weight_sum, mixed

    def answer_self(queries, peak, weight_sum, mixed):
        arrived(akv.at[pl.ds(0, N_CTX - 1)], 9)
        pairs = akv[...].astype(F32)
        scores = dot_t(queries, pairs[:, 0, :].astype(BF16))
        token = lax.broadcasted_iota(jnp.int32, (GROUP * QTOK, QTOK), 0) % QTOK
        seen = lax.broadcasted_iota(jnp.int32, (GROUP * QTOK, QTOK), 1) <= token
        scores = jnp.where(seen, scores, -jnp.inf)
        both = jnp.maximum(peak, jnp.max(scores, axis=1, keepdims=True))
        rescale = jnp.exp2((peak - both) * C2)
        probs = jnp.exp2((scores - both) * C2)
        weight_sum = weight_sum * rescale + jnp.sum(probs, axis=1, keepdims=True)
        mixed = mixed * rescale + jnp.dot(
            probs.astype(BF16), pairs[:, 1, :].astype(BF16), preferred_element_type=F32
        )
        return both, weight_sum, mixed

    def answer_scatter():
        queries, peak, weight_sum, mixed = answer_part()
        peak, weight_sum, mixed = lax.cond(
            c == 0,
            lambda: answer_self(queries, peak, weight_sum, mixed),
            lambda: (peak, weight_sum, mixed),
        )
        level = peak * C2 + jnp.log2(weight_sum)
        mixed = mixed / weight_sum
        lane = lax.broadcasted_iota(jnp.int32, (QTOK, HD), 1) // 32
        levels = jnp.zeros((QTOK, HD), F32)
        for h in range(GROUP):
            o_f[:, h, :] = mixed[h * QTOK : (h + 1) * QTOK]
            levels = jnp.where(lane == h, level[h * QTOK : (h + 1) * QTOK], levels)
        o_src[...] = o_f[...].astype(BF16)
        l_src[...] = levels.reshape(QTOK, 1, HD)
        for d in range(1, N_CTX):
            to = (c + d) % N_CTX
            send(o_src.at[to], o_recv.at[c], 10, ctx=to)
            send(l_src.at[to], l_recv.at[c], 11, ctx=to)
        o_recv[c] = o_src[c]
        l_recv[c] = l_src[c]

    def answer_merge():
        arrived(o_recv.at[pl.ds(0, N_CTX - 1)], 10)
        arrived(l_recv.at[pl.ds(0, N_CTX - 1)], 11)
        o_f[...] = o_recv[...].astype(F32)
        level = l_recv[...].reshape(N_CTX, HD)
        weight = jnp.exp2(level - jnp.max(level, axis=0, keepdims=True))
        heads = []
        for h in range(GROUP):
            part = weight[:, 32 * h : 32 * h + 1]
            mixed = jnp.sum(o_f[:, h, :] * part, axis=0, keepdims=True)
            heads.append(mixed / jnp.sum(part, axis=0, keepdims=True))
        h_src[...] = jnp.concatenate(heads, axis=0).astype(BF16)
        for d in range(1, N_CTX):
            send(h_src, h_all.at[c], 12, ctx=(c + d) % N_CTX)
        h_all[c] = h_src[...]

    def answer_project():
        arrived(h_all.at[pl.ds(0, N_CTX - 1)], 12)
        o_f[...] = h_all[...].astype(F32)
        flat = jnp.concatenate([o_f[:, h, :] for h in range(GROUP)], axis=1).astype(BF16)
        share = jnp.dot(flat, w_v[...], preferred_element_type=F32)
        p_src[...] = share.reshape(N_TP, QTOK // N_TP, HD)
        for d in range(1, N_TP):
            to = (p + d) % N_TP
            send(p_src.at[to], p_recv.at[p], 13, tp=to)
        p_recv[p] = p_src[p]
        arrived(p_recv.at[pl.ds(0, N_TP - 1)], 13)
        ans_ref[...] = jnp.sum(p_recv[...], axis=0).astype(BF16)

    for d in range(1, N_CTX):
        send(aq_ref.at[0], q_all.at[c], 8, ctx=(c + d) % N_CTX)
    near_scatter(0)
    near_scatter(1)

    @pl.when(c != 0)
    def _():
        send(ap_ref.at[0], akv.at[c], 9, ctx=0)

    @pl.when(c == 0)
    def _():
        akv[0] = ap_ref[0]

    loads[1].wait()
    own_part(0)
    own_part(1)
    own_part(2)
    z_scatter(0)
    z_scatter(1)
    own_part(3)
    answer_scatter()
    z_gather(0)
    z_gather(1)
    near_gather(0)
    answer_merge()
    near_gather(1)
    far_here(0)
    far_here(1)
    far_part()
    store = pltpu.make_async_copy(out_v, out_hbm, store_sem)
    store.start()
    loads[2].wait()
    answer_project()

    for kv in range(2):
        sent(near_cand[kv].at[pl.ds(0, 3)], kv)
        sent(z_cand[kv].at[pl.ds(0, N_Z - 1)], 2 + kv)
        sent(far.at[kv, 0, pl.ds(0, N_Z - 1)], 4 + kv)
        sent(far.at[kv, pl.ds(0, 3)], 6 + kv)
    sent(q_all.at[pl.ds(0, N_CTX - 1)], 8)

    @pl.when(c != 0)
    def _():
        sent(akv.at[0], 9)

    sent(o_recv.at[pl.ds(0, N_CTX - 1)], 10)
    sent(l_recv.at[pl.ds(0, N_CTX - 1)], 11)
    sent(h_all.at[pl.ds(0, N_CTX - 1)], 12)
    sent(p_recv.at[pl.ds(0, N_TP - 1)], 13)
    store.wait()


def on_device(
    context_query, context_pairs, anchor_block, answer_query, answer_pairs, output_weight
):
    hbm = pl.BlockSpec(memory_space=pltpu.HBM)
    any_space = pl.BlockSpec(memory_space=pl.ANY)
    vmem = pl.BlockSpec(memory_space=pltpu.VMEM)
    out, answer_output = pl.pallas_call(
        kernel,
        out_shape=(
            jax.ShapeDtypeStruct((ROWS, HD), BF16),
            jax.ShapeDtypeStruct((QTOK // N_TP, HD), BF16),
        ),
        in_specs=[pl.BlockSpec(memory_space=pltpu.SMEM), hbm, hbm, hbm, hbm, hbm],
        out_specs=(any_space, vmem),
        scratch_shapes=[
            pltpu.VMEM((ROWS, HD), BF16),
            pltpu.VMEM((2 * BLOCK, HD), BF16),
            pltpu.VMEM((2 * BLOCK, HD), F32),
            pltpu.VMEM((1, GROUP, HD), BF16),
            pltpu.VMEM((1, 2, HD), BF16),
            pltpu.VMEM((GROUP * HD, HD), BF16),
            pltpu.VMEM((ROWS, HD), BF16),
            pltpu.VMEM((2, 4, N_Z, 16, HD), BF16),
            pltpu.VMEM((4, N_Z, 16, HD), BF16),
            pltpu.VMEM((4, N_Z, 16, HD), BF16),
            pltpu.VMEM((2, N_Z, 16, HD), BF16),
            pltpu.VMEM((N_Z, 16, HD), BF16),
            pltpu.VMEM((N_Z, 16, HD), BF16),
            pltpu.VMEM((2, 4, N_Z, 16, HD), BF16),
            pltpu.VMEM((ROWS, 1), F32),
            pltpu.VMEM((ROWS, 1), F32),
            pltpu.VMEM((ROWS, HD), F32),
            pltpu.VMEM((N_CTX, GROUP, HD), BF16),
            pltpu.VMEM((N_CTX, 2, HD), BF16),
            pltpu.VMEM((N_CTX, GROUP, HD), F32),
            pltpu.VMEM((N_CTX, GROUP, HD), BF16),
            pltpu.VMEM((N_CTX, 1, HD), F32),
            pltpu.VMEM((N_CTX, GROUP, HD), BF16),
            pltpu.VMEM((N_CTX, 1, HD), F32),
            pltpu.VMEM((GROUP, HD), BF16),
            pltpu.VMEM((N_CTX, GROUP, HD), BF16),
            pltpu.VMEM((N_TP, QTOK // N_TP, HD), F32),
            pltpu.VMEM((N_TP, QTOK // N_TP, HD), F32),
            pltpu.SemaphoreType.DMA((5,)),
            pltpu.SemaphoreType.DMA,
            pltpu.SemaphoreType.DMA((14,)),
            pltpu.SemaphoreType.DMA((14,)),
        ],
        compiler_params=pltpu.CompilerParams(
            collective_id=0, has_side_effects=True, vmem_limit_bytes=60 * 1024 * 1024
        ),
        cost_estimate=pl.CostEstimate(
            flops=4 * ROWS * BLOCK * HD * 2, bytes_accessed=1 << 22, transcendentals=2 * ROWS * BLOCK
        ),
        name="two_phase_attention",
    )(
        anchor_block,
        context_query.reshape(ROWS, HD),
        context_pairs.reshape(2 * BLOCK, HD),
        answer_query,
        answer_pairs.reshape(1, 2, HD),
        output_weight,
    )
    return out.reshape(BLOCK, GROUP, HD), answer_output


def solution(mesh):
    in_specs = (
        P("ctx", "tp", None),
        P("ctx", "tp", None, None),
        P(),
        P("ctx", "tp", None),
        P("ctx", "tp", None, None),
        P("tp", "ctx"),
    )
    out_specs = (P("ctx", "tp", None), P("tp", "ctx"))
    return jax.shard_map(
        on_device, mesh=mesh, in_specs=in_specs, out_specs=out_specs, check_vma=False
    )
```

time: 817 us -> 74.8 us (0.09)
  waiting for transfers between devices: 355 us -> 0 us
  blocking collectives: 328 us -> 0 us
  other arithmetic: 76.7 us -> 0 us
  Pallas kernels: 0 us -> 70.2 us
  matrix products: 17.8 us -> 0 us
  between operations: 15.5 us -> 1.29 us
  local copies, waits for them, and re-layouts: 15.6 us -> 3.14 us
    all_gather x4 -> x0, blocking collectives: 301 us -> none  [the longest x2 145 us: merged_2(): pieces = jax.tree.map(lambda part: lax.all_gather(part, axis), value)]
    psum x1 -> x0, waiting for transfers between devices: 218 us -> none  [from_root(): return lax.psum(block, axis)]
    all_gather x1 -> x0, waiting for transfers between devices: 137 us -> none  [merged_2(): pieces = jax.tree.map(lambda part: lax.all_gather(part, axis), value)]
    pallas_call x0 -> x1, Pallas kernels: none -> 70.2 us  [on_device(): pl.pallas_call(kernel, out_shape=(jax.ShapeDtypeStruct((ROWS, HD), BF16),...]
    add x131 -> x0, other arithmetic: 69.1 us -> none  [the longest x63 67.5 us: combine_parts(): first[2] * first_rescale[..., None] + second[2] * second_rescale[..., None]]
    unnamed x1 -> x0, blocking collectives: 26.2 us -> none
    dot_general x21 -> x0, matrix products: 17.8 us -> none  [the longest x4 6.24 us: one_head(): jnp.dot(own_probs.astype(jnp.bfloat16), own_values, preferred_element_typ...]
    slice x9 -> x0, local copies, waits for them, and re-layouts: 8.23 us -> none  [the longest x5 8.22 us: merged_2(): tail = jax.tree.map(lambda part: part[1:], pieces)]
  transfers between devices with their start and end apart: 2 -> 0, of which waited for: 2 -> 0; matrix products, arithmetic and copies ran while one was open for 4% -> 0% of each run, Pallas kernels for 0% -> 0%
where the time goes in v1:
time: 74.8 us; the launch traced here: 74.6 us
  Pallas kernels  70.2 us (94%)
  local copies, waits for them, and re-layouts  3.14 us (4%)
  between operations  1.29 us (2%)
    pallas_call x1, Pallas kernels, on_device(): pl.pallas_call(kernel, out_shape=(jax.ShapeDtypeStruct((ROWS, HD), BF16),...  70.2 us
    unnamed x4, local copies, waits for them, and re-layouts  3.14 us

profile of v1, /device:TPU:1, one launch (start us, length us, event | category | flops | bytes accessed | tf_op | source)
XLA Modules:
  0.0 74.6 jit_solution(17942406020417118352)
XLA Ops:
  1.3 70.2 %two_phase_attention.1 = (bf16[4096,128]{1,0:T(8,128)(2,1)}, bf16[8,128]{1,0:T(8,128)(2,1)}) custom-call(s32[1]{0:T(128)S(6)} %copy.10.anchor_ref, bf16[4096,128]{1,0:T(8,128)(2,1)} %bitcast.5, bf16[2048,128]{1,0:T(8,128)(2,1)} %bitcast.6, bf16[1,4,128]{2,1,0:T(4,128)(2,1)} %aq_hbm.1, bf16[1,2,128]{2,1,0:T(2,128)(2,1)} %bitcast.7, bf16[512,128]{1,0:T(8,128)(2,1)} %w_hbm.1), custom_call_target="tpu_custom_call" | custom-call | flops 4294967296 | bytes 4194304 | tf_op jit(solution)/shard_map/two_phase_attention/pallas_call | solution.py:293
  71.5 0.0 copy-start
  71.5 2.6 %copy.11 = bf16[1024,4,128]{2,1,0:T(4,128)(2,1)} copy(bf16[1024,4,128]{2,1,0:T(4,128)(2,1)} %bitcast.4) | data formatting | bytes 2097152
  74.0 0.0 copy-done
  74.0 0.6 copy.12
Async XLA Ops:
  71.5 2.6 %copy-start = (bf16[8,128]{1,0:T(8,128)(2,1)S(1)}, bf16[8,128]{1,0:T(8,128)(2,1)}, u32[]{:S(2)}) copy-start(bf16[8,128]{1,0:T(8,128)(2,1)} %get-tuple-element.9) | copy-start | bytes 6148

commit v2 on v1

v2 whole, which is shorter than its diff:
```python
import functools
import math

import jax
import jax.numpy as jnp
from jax import lax
from jax.experimental import pallas as pl
from jax.experimental.pallas import tpu as pltpu
from jax.sharding import PartitionSpec as P

MESH = pl.DeviceIdType.MESH
N_CTX, N_TP, N_Z = 64, 8, 16
HD, GROUP, BLOCK, QTOK = 128, 4, 1024, 64
ROWS = BLOCK * GROUP
COLS = 1024
F32, BF16 = jnp.float32, jnp.bfloat16
C2 = HD**-0.5 * math.log2(math.e)


def dot_t(a, b):
    return lax.dot_general(a, b, (((1,), (1,)), ((), ())), preferred_element_type=F32)


def kernel(
    anchor_ref, q_hbm, pairs_hbm, aq_hbm, ap_hbm, w_hbm,
    out_ref, ans_ref,
    q_v, pairs_v, pairs_f, w_v, own_k, own_vt,
    cand_0, cand_1, z_src, z_cand_0, z_cand_1, far_0, far_1, far_f, far_k, far_vt,
    m_s, l_s, acc_s,
    q_all, akv, o_src, l_src, o_recv, l_recv,
    o2_src, l2_src, o2_recv, l2_recv, h_src, h_all, h_f, p_src, p_recv,
    load_sem, send_sem, recv_sem,
):
    c = lax.axis_index("ctx")
    p = lax.axis_index("tp")
    y, z, k = c // 32, (c // 2) % N_Z, c % 2
    rank = 2 * y + k
    z_hi, z_lo = z // 4, z % 4
    local = 4 * z_lo + rank

    def ctx_at(y, z, k):
        return (y * N_Z + z) * 2 + k

    anchor = anchor_ref[0]
    a_rank, a_z = 2 * (anchor // 32) + anchor % 2, (anchor // 2) % N_Z
    is_anchor = anchor == c

    barrier = pltpu.get_barrier_semaphore()
    for d in range(1, N_CTX):
        pl.semaphore_signal(barrier, inc=1, device_id={"ctx": (c + d) % N_CTX}, device_id_type=MESH)
    for d in range(1, N_TP):
        pl.semaphore_signal(barrier, inc=1, device_id={"tp": (p + d) % N_TP}, device_id_type=MESH)
    loads = [
        pltpu.make_async_copy(pairs_hbm, pairs_v, load_sem.at[0]),
        pltpu.make_async_copy(q_hbm, q_v, load_sem.at[1]),
        pltpu.make_async_copy(w_hbm, w_v, load_sem.at[2]),
        pltpu.make_async_copy(aq_hbm.at[0], q_all.at[c], load_sem.at[3]),
    ]
    for load in loads:
        load.start()
    pl.semaphore_wait(barrier, N_CTX - 1 + N_TP - 1)

    def send(src, dst, sem, **device):
        pltpu.make_async_remote_copy(
            src_ref=src, dst_ref=dst, send_sem=send_sem.at[sem], recv_sem=recv_sem.at[sem],
            device_id=device, device_id_type=MESH,
        ).start()

    def arrived(ref, sem):
        pltpu.make_async_copy(ref, ref, recv_sem.at[sem]).wait()

    def sent(ref, sem):
        pltpu.make_async_copy(ref, ref, send_sem.at[sem]).wait()

    near = [(y, 1 - k), (1 - y, k), (1 - y, 1 - k)]
    cand, z_cand, far = (cand_0, cand_1), (z_cand_0, z_cand_1), (far_0, far_1)

    def near_scatter(half):
        for to_y, to_k in near:
            to = 2 * to_y + to_k
            send(pairs_hbm.at[to, half], cand[half].at[rank], half, ctx=ctx_at(to_y, z, to_k))

    def z_scatter(half):
        cand[half][rank] = pairs_v[rank, half]
        arrived(cand[half].at[pl.ds(0, 3)], half)
        z_src[half] = cand[half][a_rank]
        for d in range(1, N_Z):
            to = (z + d) % N_Z
            send(z_src.at[half, to], z_cand[half].at[z], 2 + half, ctx=ctx_at(y, to, k))
        z_cand[half][z] = z_src[half, z]

    def z_gather(half):
        arrived(z_cand[half].at[pl.ds(0, N_Z - 1)], 2 + half)
        far[half][rank, z] = z_cand[half][a_z]
        for d in range(1, N_Z):
            to = (z + d) % N_Z
            send(far[half].at[rank, z], far[half].at[rank, z], 4 + half, ctx=ctx_at(y, to, k))

    def near_gather(half):
        arrived(far[half].at[0, pl.ds(0, N_Z - 1)], 4 + half)
        for to_y, to_k in near:
            send(far[half].at[rank], far[half].at[rank], 6 + half, ctx=ctx_at(to_y, z, to_k))

    def own_part(i):
        cols = slice(i * COLS, (i + 1) * COLS)
        scores = dot_t(own_k[0 : (i + 1) * 256, :], q_v[cols, :])
        token = lax.broadcasted_iota(jnp.int32, (256, COLS), 1) // GROUP
        seen = lax.broadcasted_iota(jnp.int32, (256, COLS), 0) <= token
        last = jnp.where(seen, scores[i * 256 :], -jnp.inf)
        scores = jnp.concatenate([scores[: i * 256], last], axis=0) if i else last
        peak = jnp.max(scores, axis=0, keepdims=True)
        probs = jnp.exp2((scores - peak) * C2)
        m_s[:, cols] = peak
        l_s[:, cols] = jnp.sum(probs, axis=0, keepdims=True)
        acc_s[:, cols] = jnp.dot(
            own_vt[:, 0 : (i + 1) * 256], probs.astype(BF16), preferred_element_type=F32
        )

    def far_here(half):
        arrived(far[half].at[pl.ds(0, 3)], 6 + half)
        far_f[...] = far[half][...].reshape(BLOCK, HD).astype(F32)
        far_k[...] = far_f[pl.ds(0, BLOCK // 2, stride=2), :].astype(BF16)
        far_vt[...] = far_f[pl.ds(1, BLOCK // 2, stride=2), :].astype(BF16).T

    def far_part(blocks, last):
        far_weight = jnp.where(is_anchor, 0.0, 1.0).astype(F32)
        for i in blocks:
            cols = slice(i * COLS, (i + 1) * COLS)
            scores = dot_t(far_k[...], q_v[cols, :])
            before = m_s[:, cols]
            peak = jnp.maximum(before, jnp.max(scores, axis=0, keepdims=True))
            probs = jnp.exp2((scores - peak) * C2)
            rescale = jnp.where(is_anchor, 1.0, jnp.exp2((before - peak) * C2))
            weight_sum = l_s[:, cols] * rescale + far_weight * jnp.sum(probs, axis=0, keepdims=True)
            mixed = acc_s[:, cols] * rescale + far_weight * jnp.dot(
                far_vt[...], probs.astype(BF16), preferred_element_type=F32
            )
            if last:
                out_ref[cols, :] = (mixed / weight_sum).T.astype(BF16)
            else:
                m_s[:, cols] = peak
                l_s[:, cols] = weight_sum
                acc_s[:, cols] = mixed


    def answer_self(queries, peak, weight_sum, mixed):
        arrived(akv.at[pl.ds(0, N_CTX - 1)], 9)
        pairs = akv[...].astype(F32)
        scores = dot_t(pairs[:, 0, :].astype(BF16), queries)
        token = lax.broadcasted_iota(jnp.int32, (QTOK, GROUP * QTOK), 1) // GROUP
        seen = lax.broadcasted_iota(jnp.int32, (QTOK, GROUP * QTOK), 0) <= token
        scores = jnp.where(seen, scores, -jnp.inf)
        both = jnp.maximum(peak, jnp.max(scores, axis=0, keepdims=True))
        rescale = jnp.exp2((peak - both) * C2)
        probs = jnp.exp2((scores - both) * C2)
        weight_sum = weight_sum * rescale + jnp.sum(probs, axis=0, keepdims=True)
        mixed = mixed * rescale + jnp.dot(
            pairs[:, 1, :].T.astype(BF16), probs.astype(BF16), preferred_element_type=F32
        )
        return both, weight_sum, mixed

    def local_peers():
        for d in range(1, 16):
            to_z, to_rank = (z_lo + d // 4) % 4, (rank + d) % 4
            yield 4 * to_z + to_rank, ctx_at(to_rank // 2, 4 * z_hi + to_z, to_rank % 2)

    def answer_part():
        arrived(q_all.at[pl.ds(0, N_CTX - 1)], 8)
        queries = q_all[...].astype(F32).reshape(GROUP * QTOK, HD).astype(BF16)
        scores = dot_t(own_k[...], queries)
        peak = jnp.max(scores, axis=0, keepdims=True)
        probs = jnp.exp2((scores - peak) * C2)
        weight_sum = jnp.sum(probs, axis=0, keepdims=True)
        mixed = jnp.dot(own_vt[...], probs.astype(BF16), preferred_element_type=F32)
        peak, weight_sum, mixed = lax.cond(
            c == 0,
            lambda: answer_self(queries, peak, weight_sum, mixed),
            lambda: (peak, weight_sum, mixed),
        )
        l_src[...] = peak * C2 + jnp.log2(weight_sum)
        o_src[...] = (mixed / weight_sum).T.astype(BF16).reshape(16, 16, HD)
        for to, device in local_peers():
            send(o_src.at[to], o_recv.at[local], 10, ctx=device)
            send(l_src, l_recv.at[local], 11, ctx=device)
        o_recv[local] = o_src[local]
        l_recv[local] = l_src[...]

    def merged(parts, levels, first_lane):
        width = levels[0].shape[1]
        row = lax.broadcasted_iota(jnp.int32, (16, width), 0) + first_lane
        mine = lax.broadcasted_iota(jnp.int32, (16, width), 1) == row
        columns = [
            jnp.sum(jnp.where(mine, level, 0.0), axis=1, keepdims=True) for level in levels
        ]
        peak = functools.reduce(jnp.maximum, columns)
        weights = [jnp.exp2(column - peak) for column in columns]
        weight_sum = functools.reduce(jnp.add, weights)
        mixed = functools.reduce(
            jnp.add, [part.astype(F32) * weight for part, weight in zip(parts, weights)]
        )
        return mixed / weight_sum, peak + jnp.log2(weight_sum)

    def answer_local():
        arrived(o_recv.at[pl.ds(0, 15)], 10)
        arrived(l_recv.at[pl.ds(0, 15)], 11)
        mixed, level = merged(
            [o_recv[n] for n in range(16)], [l_recv[n] for n in range(16)], 16 * local
        )
        o2_src[...] = mixed.astype(BF16)
        row = lax.broadcasted_iota(jnp.int32, (16, HD), 0)
        lane = lax.broadcasted_iota(jnp.int32, (16, HD), 1)
        l2_src[...] = jnp.sum(jnp.where(row == lane, level, 0.0), axis=0, keepdims=True)
        for d in range(1, 4):
            to = ctx_at(y, 4 * ((z_hi + d) % 4) + z_lo, k)
            send(o2_src, o2_recv.at[z_hi], 12, ctx=to)
            send(l2_src, l2_recv.at[z_hi], 13, ctx=to)
        o2_recv[z_hi] = o2_src[...]
        l2_recv[z_hi] = l2_src[...]

    def answer_heads():
        arrived(o2_recv.at[pl.ds(0, 3)], 12)
        arrived(l2_recv.at[pl.ds(0, 3)], 13)
        mixed, _ = merged([o2_recv[n] for n in range(4)], [l2_recv[n] for n in range(4)], 0)
        h_src[...] = mixed.astype(BF16)
        for _, device in local_peers():
            send(h_src, h_all.at[local], 14, ctx=device)
        h_all[local] = h_src[...]

    def answer_project():
        arrived(h_all.at[pl.ds(0, 15)], 14)
        h_f[...] = h_all[...].reshape(GROUP * QTOK, HD).astype(F32)
        flat = jnp.concatenate(
            [h_f[pl.ds(h, QTOK, stride=GROUP), :] for h in range(GROUP)], axis=1
        ).astype(BF16)
        share = jnp.dot(flat, w_v[...], preferred_element_type=F32)
        p_src[...] = share.reshape(N_TP, QTOK // N_TP, HD)
        for d in range(1, N_TP):
            to = (p + d) % N_TP
            send(p_src.at[to], p_recv.at[p], 15, tp=to)
        p_recv[p] = p_src[p]

    def answer_sum():
        arrived(p_recv.at[pl.ds(0, N_TP - 1)], 15)
        ans_ref[...] = jnp.sum(p_recv[...], axis=0).astype(BF16)

    for d in range(1, N_CTX):
        send(aq_hbm.at[0], q_all.at[c], 8, ctx=(c + d) % N_CTX)
    near_scatter(0)
    near_scatter(1)

    @pl.when(c != 0)
    def _():
        send(ap_hbm.at[0], akv.at[c], 9, ctx=0)

    @pl.when(c == 0)
    def _():
        own = pltpu.make_async_copy(ap_hbm.at[0], akv.at[0], load_sem.at[4])
        own.start()
        own.wait()

    loads[0].wait()
    pairs_f[...] = pairs_v[...].reshape(2 * BLOCK, HD).astype(F32)
    own_k[...] = pairs_f[pl.ds(0, BLOCK, stride=2), :].astype(BF16)
    own_vt[...] = pairs_f[pl.ds(1, BLOCK, stride=2), :].astype(BF16).T
    loads[1].wait()
    loads[3].wait()
    own_part(0)
    own_part(1)
    own_part(2)
    z_scatter(0)
    own_part(3)
    z_scatter(1)
    answer_part()
    z_gather(0)
    z_gather(1)
    answer_local()
    near_gather(0)
    near_gather(1)
    answer_heads()
    far_here(0)
    far_part(range(4), False)
    far_here(1)
    far_part(range(2), True)
    loads[2].wait()
    answer_project()
    far_part(range(2, 4), True)
    answer_sum()

    for half in range(2):
        sent(cand[half].at[pl.ds(0, 3)], half)
        sent(z_cand[half].at[pl.ds(0, N_Z - 1)], 2 + half)
        sent(far[half].at[0, pl.ds(0, N_Z - 1)], 4 + half)
        sent(far[half].at[pl.ds(0, 3)], 6 + half)
    sent(q_all.at[pl.ds(0, N_CTX - 1)], 8)

    @pl.when(c != 0)
    def _():
        sent(akv.at[0], 9)

    sent(o_recv.at[pl.ds(0, 15)], 10)
    sent(l_recv.at[pl.ds(0, 15)], 11)
    sent(o2_recv.at[pl.ds(0, 3)], 12)
    sent(l2_recv.at[pl.ds(0, 3)], 13)
    sent(h_all.at[pl.ds(0, 15)], 14)
    sent(p_recv.at[pl.ds(0, N_TP - 1)], 15)


def in_hbm(array):
    return pltpu.with_memory_space_constraint(array, pltpu.HBM)


def on_device(
    context_query, context_pairs, anchor_block, answer_query, answer_pairs, output_weight
):
    hbm = pl.BlockSpec(memory_space=pltpu.HBM)
    vmem = pl.BlockSpec(memory_space=pltpu.VMEM)
    out, answer_output = pl.pallas_call(
        kernel,
        out_shape=(
            jax.ShapeDtypeStruct((ROWS, HD), BF16),
            jax.ShapeDtypeStruct((QTOK // N_TP, HD), BF16),
        ),
        in_specs=[pl.BlockSpec(memory_space=pltpu.SMEM), hbm, hbm, hbm, hbm, hbm],
        out_specs=(vmem, vmem),
        scratch_shapes=[
            pltpu.VMEM((ROWS, HD), BF16),
            pltpu.VMEM((4, 2, N_Z, 16, HD), BF16),
            pltpu.VMEM((2 * BLOCK, HD), F32),
            pltpu.VMEM((GROUP * HD, HD), BF16),
            pltpu.VMEM((BLOCK, HD), BF16),
            pltpu.VMEM((HD, BLOCK), BF16),
            pltpu.VMEM((4, N_Z, 16, HD), BF16),
            pltpu.VMEM((4, N_Z, 16, HD), BF16),
            pltpu.VMEM((2, N_Z, 16, HD), BF16),
            pltpu.VMEM((N_Z, 16, HD), BF16),
            pltpu.VMEM((N_Z, 16, HD), BF16),
            pltpu.VMEM((4, N_Z, 16, HD), BF16),
            pltpu.VMEM((4, N_Z, 16, HD), BF16),
            pltpu.VMEM((BLOCK, HD), F32),
            pltpu.VMEM((BLOCK // 2, HD), BF16),
            pltpu.VMEM((HD, BLOCK // 2), BF16),
            pltpu.VMEM((1, ROWS), F32),
            pltpu.VMEM((1, ROWS), F32),
            pltpu.VMEM((HD, ROWS), F32),
            pltpu.VMEM((N_CTX, GROUP, HD), BF16),
            pltpu.VMEM((N_CTX, 2, HD), BF16),
            pltpu.VMEM((16, 16, HD), BF16),
            pltpu.VMEM((1, GROUP * QTOK), F32),
            pltpu.VMEM((16, 16, HD), BF16),
            pltpu.VMEM((16, 1, GROUP * QTOK), F32),
            pltpu.VMEM((16, HD), BF16),
            pltpu.VMEM((1, HD), F32),
            pltpu.VMEM((4, 16, HD), BF16),
            pltpu.VMEM((4, 1, HD), F32),
            pltpu.VMEM((16, HD), BF16),
            pltpu.VMEM((16, 16, HD), BF16),
            pltpu.VMEM((GROUP * QTOK, HD), F32),
            pltpu.VMEM((N_TP, QTOK // N_TP, HD), F32),
            pltpu.VMEM((N_TP, QTOK // N_TP, HD), F32),
            pltpu.SemaphoreType.DMA((5,)),
            pltpu.SemaphoreType.DMA((16,)),
            pltpu.SemaphoreType.DMA((16,)),
        ],
        compiler_params=pltpu.CompilerParams(
            collective_id=0, has_side_effects=True, vmem_limit_bytes=40 * 1024 * 1024
        ),
        cost_estimate=pl.CostEstimate(
            flops=4 * ROWS * BLOCK * HD * 2, bytes_accessed=1 << 22, transcendentals=2 * ROWS * BLOCK
        ),
        name="two_phase_attention",
    )(
        anchor_block,
        in_hbm(context_query.reshape(ROWS, HD)),
        in_hbm(context_pairs.reshape(4, 2, N_Z, 16, HD)),
        in_hbm(answer_query),
        in_hbm(answer_pairs.reshape(1, 2, HD)),
        in_hbm(output_weight),
    )
    return out.reshape(BLOCK, GROUP, HD), answer_output


def solution(mesh):
    in_specs = (
        P("ctx", "tp", None),
        P("ctx", "tp", None, None),
        P(),
        P("ctx", "tp", None),
        P("ctx", "tp", None, None),
        P("tp", "ctx"),
    )
    out_specs = (P("ctx", "tp", None), P("tp", "ctx"))
    return jax.shard_map(
        on_device, mesh=mesh, in_specs=in_specs, out_specs=out_specs, check_vma=False
    )
```

time: 74.8 us -> 61 us (0.82)
  Pallas kernels: 70.2 us -> 58.1 us
  local copies, waits for them, and re-layouts: 3.14 us -> 1.55 us
    pallas_call x1, Pallas kernels: 70.2 us -> 58.1 us  [on_device(): pl.pallas_call(kernel, out_shape=(jax.ShapeDtypeStruct((ROWS, HD), BF16),...]
    unnamed x4 -> x2, local copies, waits for them, and re-layouts: 3.14 us -> 1.55 us
where the time goes in v2:
time: 61 us; the launch traced here: 60.9 us
  Pallas kernels  58.1 us (95%)
  local copies, waits for them, and re-layouts  1.55 us (3%)
  between operations  1.29 us (2%)
    pallas_call x1, Pallas kernels, on_device(): pl.pallas_call(kernel, out_shape=(jax.ShapeDtypeStruct((ROWS, HD), BF16),...  58.1 us
    unnamed x2, local copies, waits for them, and re-layouts  1.55 us

profile of v2, /device:TPU:1, one launch (start us, length us, event | category | flops | bytes accessed | tf_op | source)
XLA Modules:
  0.0 60.9 jit_solution(11724153870486111995)
XLA Ops:
  1.3 58.1 %two_phase_attention.1 = (bf16[4096,128]{1,0:T(8,128)(2,1)S(1)}, bf16[8,128]{1,0:T(8,128)(2,1)S(1)}) custom-call(s32[1]{0:T(128)S(6)} %copy.10.anchor_ref, bf16[4096,128]{1,0:T(8,128)(2,1)} %bitcast.5, bf16[4,2,16,16,128]{4,3,2,1,0:T(8,128)(2,1)} %bitcast.6, bf16[1,4,128]{2,1,0:T(4,128)(2,1)} %aq_hbm.1, bf16[1,2,128]{2,1,0:T(2,128)(2,1)} %bitcast.7, ...), custom_call_target="tpu_custom_call" | custom-call | flops 4294967296 | bytes 4194304 | tf_op jit(solution)/shard_map/two_phase_attention/pallas_call | solution.py:317
  59.3 1.0 %copy.11 = bf16[1024,4,128]{2,1,0:T(4,128)(2,1)} copy(bf16[1024,4,128]{2,1,0:T(4,128)(2,1)S(1)} %bitcast.4) | data formatting | bytes 2097152
  60.3 0.6 copy.12

commit v3 on v2

--- a/solution.py
+++ b/solution.py
@@ -29,7 +29,7 @@
     m_s, l_s, acc_s,
     q_all, akv, o_src, l_src, o_recv, l_recv,
     o2_src, l2_src, o2_recv, l2_recv, h_src, h_all, h_f, p_src, p_recv,
-    load_sem, send_sem, recv_sem,
+    here_sem, load_sem, send_sem, recv_sem,
 ):
     c = lax.axis_index("ctx")
     p = lax.axis_index("tp")
@@ -41,24 +41,34 @@
     def ctx_at(y, z, k):
         return (y * N_Z + z) * 2 + k
 
+    def signal(sem, **device):
+        pl.semaphore_signal(sem, inc=1, device_id=device, device_id_type=MESH)
+
+    def signal_z(sem, distance):
+        signal(sem, ctx=ctx_at(y, (z + distance) % N_Z, k))
+        signal(sem, ctx=ctx_at(y, (z + N_Z - distance) % N_Z, k))
+
     anchor = anchor_ref[0]
     a_rank, a_z = 2 * (anchor // 32) + anchor % 2, (anchor // 2) % N_Z
     is_anchor = anchor == c
 
+    near = [(y, 1 - k), (1 - y, k), (1 - y, 1 - k)]
     barrier = pltpu.get_barrier_semaphore()
-    for d in range(1, N_CTX):
-        pl.semaphore_signal(barrier, inc=1, device_id={"ctx": (c + d) % N_CTX}, device_id_type=MESH)
+    for to_y, to_k in near:
+        signal(barrier, ctx=ctx_at(to_y, z, to_k))
+    signal_z(barrier, 1)
     for d in range(1, N_TP):
-        pl.semaphore_signal(barrier, inc=1, device_id={"tp": (p + d) % N_TP}, device_id_type=MESH)
+        signal(barrier, tp=(p + d) % N_TP)
     loads = [
         pltpu.make_async_copy(pairs_hbm, pairs_v, load_sem.at[0]),
         pltpu.make_async_copy(q_hbm, q_v, load_sem.at[1]),
         pltpu.make_async_copy(w_hbm, w_v, load_sem.at[2]),
         pltpu.make_async_copy(aq_hbm.at[0], q_all.at[c], load_sem.at[3]),
+        pltpu.make_async_copy(ap_hbm.at[0], akv.at[c], load_sem.at[4]),
     ]
     for load in loads:
         load.start()
-    pl.semaphore_wait(barrier, N_CTX - 1 + N_TP - 1)
+    pl.semaphore_wait(barrier, 3 + 2 + N_TP - 1)
 
     def send(src, dst, sem, **device):
         pltpu.make_async_remote_copy(
@@ -72,7 +82,6 @@
     def sent(ref, sem):
         pltpu.make_async_copy(ref, ref, send_sem.at[sem]).wait()
 
-    near = [(y, 1 - k), (1 - y, k), (1 - y, 1 - k)]
     cand, z_cand, far = (cand_0, cand_1), (z_cand_0, z_cand_1), (far_0, far_1)
 
     def near_scatter(half):
@@ -144,7 +153,7 @@
 
 
     def answer_self(queries, peak, weight_sum, mixed):
-        arrived(akv.at[pl.ds(0, N_CTX - 1)], 9)
+        arrived(akv.at[pl.ds(0, 4 * (N_Z - 1))], 9)
         pairs = akv[...].astype(F32)
         scores = dot_t(pairs[:, 0, :].astype(BF16), queries)
         token = lax.broadcasted_iota(jnp.int32, (QTOK, GROUP * QTOK), 1) // GROUP
@@ -164,8 +173,30 @@
             to_z, to_rank = (z_lo + d // 4) % 4, (rank + d) % 4
             yield 4 * to_z + to_rank, ctx_at(to_rank // 2, 4 * z_hi + to_z, to_rank % 2)
 
+    def answer_near():
+        for to_y, to_k in near:
+            to = ctx_at(to_y, z, to_k)
+            send(aq_hbm.at[0], q_all.at[c], 16, ctx=to)
+            send(ap_hbm.at[0], akv.at[c], 17, ctx=to)
+
+    def answer_gather():
+        loads[3].wait()
+        loads[4].wait()
+        arrived(q_all.at[pl.ds(0, 3)], 16)
+        arrived(akv.at[pl.ds(0, 3)], 17)
+        tokens = [pl.ds(2 * z, 2), pl.ds(2 * (N_Z + z), 2)]
+        for d in range(1, N_Z):
+            to = ctx_at(y, (z + d) % N_Z, k)
+            for two in tokens:
+                send(q_all.at[two], q_all.at[two], 8, ctx=to)
+
+        @pl.when((rank == 0) & (z != 0))
+        def _():
+            for two in tokens:
+                send(akv.at[two], akv.at[two], 9, ctx=0)
+
     def answer_part():
-        arrived(q_all.at[pl.ds(0, N_CTX - 1)], 8)
+        arrived(q_all.at[pl.ds(0, 4 * (N_Z - 1))], 8)
         queries = q_all[...].astype(F32).reshape(GROUP * QTOK, HD).astype(BF16)
         scores = dot_t(own_k[...], queries)
         peak = jnp.max(scores, axis=0, keepdims=True)
@@ -243,30 +274,24 @@
         arrived(p_recv.at[pl.ds(0, N_TP - 1)], 15)
         ans_ref[...] = jnp.sum(p_recv[...], axis=0).astype(BF16)
 
-    for d in range(1, N_CTX):
-        send(aq_hbm.at[0], q_all.at[c], 8, ctx=(c + d) % N_CTX)
     near_scatter(0)
+    signal_z(here_sem.at[0], 1)
+    answer_near()
     near_scatter(1)
-
-    @pl.when(c != 0)
-    def _():
-        send(ap_hbm.at[0], akv.at[c], 9, ctx=0)
-
-    @pl.when(c == 0)
-    def _():
-        own = pltpu.make_async_copy(ap_hbm.at[0], akv.at[0], load_sem.at[4])
-        own.start()
-        own.wait()
-
     loads[0].wait()
     pairs_f[...] = pairs_v[...].reshape(2 * BLOCK, HD).astype(F32)
     own_k[...] = pairs_f[pl.ds(0, BLOCK, stride=2), :].astype(BF16)
     own_vt[...] = pairs_f[pl.ds(1, BLOCK, stride=2), :].astype(BF16).T
     loads[1].wait()
-    loads[3].wait()
+    pl.semaphore_wait(here_sem.at[0], 2)
+    signal_z(here_sem.at[1], 2)
     own_part(0)
     own_part(1)
+    pl.semaphore_wait(here_sem.at[1], 2)
+    signal_z(here_sem.at[2], 4)
     own_part(2)
+    pl.semaphore_wait(here_sem.at[2], 2)
+    answer_gather()
     z_scatter(0)
     own_part(3)
     z_scatter(1)
@@ -291,11 +316,13 @@
         sent(z_cand[half].at[pl.ds(0, N_Z - 1)], 2 + half)
         sent(far[half].at[0, pl.ds(0, N_Z - 1)], 4 + half)
         sent(far[half].at[pl.ds(0, 3)], 6 + half)
-    sent(q_all.at[pl.ds(0, N_CTX - 1)], 8)
-
-    @pl.when(c != 0)
+    sent(q_all.at[pl.ds(0, 3)], 16)
+    sent(akv.at[pl.ds(0, 3)], 17)
+    sent(q_all.at[pl.ds(0, 4 * (N_Z - 1))], 8)
+
+    @pl.when((rank == 0) & (z != 0))
     def _():
-        sent(akv.at[0], 9)
+        sent(akv.at[pl.ds(0, 4)], 9)
 
     sent(o_recv.at[pl.ds(0, 15)], 10)
     sent(l_recv.at[pl.ds(0, 15)], 11)
@@ -357,9 +384,10 @@
             pltpu.VMEM((GROUP * QTOK, HD), F32),
             pltpu.VMEM((N_TP, QTOK // N_TP, HD), F32),
             pltpu.VMEM((N_TP, QTOK // N_TP, HD), F32),
+            pltpu.SemaphoreType.REGULAR((3,)),
             pltpu.SemaphoreType.DMA((5,)),
-            pltpu.SemaphoreType.DMA((16,)),
-            pltpu.SemaphoreType.DMA((16,)),
+            pltpu.SemaphoreType.DMA((18,)),
+            pltpu.SemaphoreType.DMA((18,)),
         ],
         compiler_params=pltpu.CompilerParams(
             collective_id=0, has_side_effects=True, vmem_limit_bytes=40 * 1024 * 1024

time: 61 us -> 58.4 us (0.957)
  Pallas kernels: 58.1 us -> 55.4 us
    pallas_call x1, Pallas kernels: 58.1 us -> 55.4 us  [on_device(): pl.pallas_call(kernel, out_shape=(jax.ShapeDtypeStruct((ROWS, HD), BF16),...]
where the time goes in v3:
time: 58.4 us; the launch traced here: 58.3 us
  Pallas kernels  55.4 us (95%)
  local copies, waits for them, and re-layouts  1.55 us (3%)
  between operations  1.29 us (2%)
    pallas_call x1, Pallas kernels, on_device(): pl.pallas_call(kernel, out_shape=(jax.ShapeDtypeStruct((ROWS, HD), BF16),...  55.4 us
    unnamed x2, local copies, waits for them, and re-layouts  1.55 us

profile of v3, /device:TPU:1, one launch (start us, length us, event | category | flops | bytes accessed | tf_op | source)
XLA Modules:
  0.0 58.3 jit_solution(8844351102533501444)
XLA Ops:
  1.3 55.4 %two_phase_attention.1 = (bf16[4096,128]{1,0:T(8,128)(2,1)S(1)}, bf16[8,128]{1,0:T(8,128)(2,1)S(1)}) custom-call(s32[1]{0:T(128)S(6)} %copy.10.anchor_ref, bf16[4096,128]{1,0:T(8,128)(2,1)} %bitcast.5, bf16[4,2,16,16,128]{4,3,2,1,0:T(8,128)(2,1)} %bitcast.6, bf16[1,4,128]{2,1,0:T(4,128)(2,1)} %aq_hbm.1, bf16[1,2,128]{2,1,0:T(2,128)(2,1)} %bitcast.7, ...), custom_call_target="tpu_custom_call" | custom-call | flops 4294967296 | bytes 4194304 | tf_op jit(solution)/shard_map/two_phase_attention/pallas_call | solution.py:344
  56.7 1.0 %copy.11 = bf16[1024,4,128]{2,1,0:T(4,128)(2,1)} copy(bf16[1024,4,128]{2,1,0:T(4,128)(2,1)S(1)} %bitcast.4) | data formatting | bytes 2097152
  57.7 0.6 copy.12

commit v4 on v3

--- a/solution.py
+++ b/solution.py
@@ -56,7 +56,8 @@
     barrier = pltpu.get_barrier_semaphore()
     for to_y, to_k in near:
         signal(barrier, ctx=ctx_at(to_y, z, to_k))
-    signal_z(barrier, 1)
+    for distance in (1, 2):
+        signal_z(barrier, distance)
     for d in range(1, N_TP):
         signal(barrier, tp=(p + d) % N_TP)
     loads = [
@@ -68,7 +69,7 @@
     ]
     for load in loads:
         load.start()
-    pl.semaphore_wait(barrier, 3 + 2 + N_TP - 1)
+    pl.semaphore_wait(barrier, 3 + 4 + N_TP - 1)
 
     def send(src, dst, sem, **device):
         pltpu.make_async_remote_copy(
@@ -132,20 +133,19 @@
         far_vt[...] = far_f[pl.ds(1, BLOCK // 2, stride=2), :].astype(BF16).T
 
     def far_part(blocks, last):
-        far_weight = jnp.where(is_anchor, 0.0, 1.0).astype(F32)
         for i in blocks:
             cols = slice(i * COLS, (i + 1) * COLS)
             scores = dot_t(far_k[...], q_v[cols, :])
             before = m_s[:, cols]
             peak = jnp.maximum(before, jnp.max(scores, axis=0, keepdims=True))
-            probs = jnp.exp2((scores - peak) * C2)
+            probs = jnp.exp2((scores - jnp.where(is_anchor, 1e38, peak)) * C2)
             rescale = jnp.where(is_anchor, 1.0, jnp.exp2((before - peak) * C2))
-            weight_sum = l_s[:, cols] * rescale + far_weight * jnp.sum(probs, axis=0, keepdims=True)
-            mixed = acc_s[:, cols] * rescale + far_weight * jnp.dot(
+            weight_sum = l_s[:, cols] * rescale + jnp.sum(probs, axis=0, keepdims=True)
+            mixed = acc_s[:, cols] * rescale + jnp.dot(
                 far_vt[...], probs.astype(BF16), preferred_element_type=F32
             )
             if last:
-                out_ref[cols, :] = (mixed / weight_sum).T.astype(BF16)
+                out_ref[cols, :] = (mixed * (1.0 / weight_sum)).T.astype(BF16)
             else:
                 m_s[:, cols] = peak
                 l_s[:, cols] = weight_sum
@@ -209,7 +209,7 @@
             lambda: (peak, weight_sum, mixed),
         )
         l_src[...] = peak * C2 + jnp.log2(weight_sum)
-        o_src[...] = (mixed / weight_sum).T.astype(BF16).reshape(16, 16, HD)
+        o_src[...] = (mixed * (1.0 / weight_sum)).T.astype(BF16).reshape(16, 16, HD)
         for to, device in local_peers():
             send(o_src.at[to], o_recv.at[local], 10, ctx=device)
             send(l_src, l_recv.at[local], 11, ctx=device)
@@ -275,7 +275,7 @@
         ans_ref[...] = jnp.sum(p_recv[...], axis=0).astype(BF16)
 
     near_scatter(0)
-    signal_z(here_sem.at[0], 1)
+    signal_z(here_sem.at[0], 2)
     answer_near()
     near_scatter(1)
     loads[0].wait()
@@ -284,17 +284,15 @@
     own_vt[...] = pairs_f[pl.ds(1, BLOCK, stride=2), :].astype(BF16).T
     loads[1].wait()
     pl.semaphore_wait(here_sem.at[0], 2)
-    signal_z(here_sem.at[1], 2)
+    signal_z(here_sem.at[1], 4)
     own_part(0)
     own_part(1)
+    own_part(2)
     pl.semaphore_wait(here_sem.at[1], 2)
-    signal_z(here_sem.at[2], 4)
-    own_part(2)
-    pl.semaphore_wait(here_sem.at[2], 2)
     answer_gather()
     z_scatter(0)
+    z_scatter(1)
     own_part(3)
-    z_scatter(1)
     answer_part()
     z_gather(0)
     z_gather(1)
@@ -304,11 +302,10 @@
     answer_heads()
     far_here(0)
     far_part(range(4), False)
-    far_here(1)
-    far_part(range(2), True)
     loads[2].wait()
     answer_project()
-    far_part(range(2, 4), True)
+    far_here(1)
+    far_part(range(4), True)
     answer_sum()
 
     for half in range(2):
@@ -384,7 +381,7 @@
             pltpu.VMEM((GROUP * QTOK, HD), F32),
             pltpu.VMEM((N_TP, QTOK // N_TP, HD), F32),
             pltpu.VMEM((N_TP, QTOK // N_TP, HD), F32),
-            pltpu.SemaphoreType.REGULAR((3,)),
+            pltpu.SemaphoreType.REGULAR((2,)),
             pltpu.SemaphoreType.DMA((5,)),
             pltpu.SemaphoreType.DMA((18,)),
             pltpu.SemaphoreType.DMA((18,)),

time: 58.4 us -> 57.3 us (0.981)
  Pallas kernels: 55.4 us -> 54.4 us
    pallas_call x1, Pallas kernels: 55.4 us -> 54.4 us  [on_device(): pl.pallas_call(kernel, out_shape=(jax.ShapeDtypeStruct((ROWS, HD), BF16),...]
where the time goes in v4:
time: 57.3 us; the launch traced here: 57.2 us
  Pallas kernels  54.4 us (95%)
  local copies, waits for them, and re-layouts  1.55 us (3%)
  between operations  1.29 us (2%)
    pallas_call x1, Pallas kernels, on_device(): pl.pallas_call(kernel, out_shape=(jax.ShapeDtypeStruct((ROWS, HD), BF16),...  54.4 us
    unnamed x2, local copies, waits for them, and re-layouts  1.55 us

profile of v4, /device:TPU:1, one launch (start us, length us, event | category | flops | bytes accessed | tf_op | source)
XLA Modules:
  0.0 57.2 jit_solution(5990132914156649761)
XLA Ops:
  1.3 54.4 %two_phase_attention.1 = (bf16[4096,128]{1,0:T(8,128)(2,1)S(1)}, bf16[8,128]{1,0:T(8,128)(2,1)S(1)}) custom-call(s32[1]{0:T(128)S(6)} %copy.10.anchor_ref, bf16[4096,128]{1,0:T(8,128)(2,1)} %bitcast.5, bf16[4,2,16,16,128]{4,3,2,1,0:T(8,128)(2,1)} %bitcast.6, bf16[1,4,128]{2,1,0:T(4,128)(2,1)} %aq_hbm.1, bf16[1,2,128]{2,1,0:T(2,128)(2,1)} %bitcast.7, ...), custom_call_target="tpu_custom_call" | custom-call | flops 4294967296 | bytes 4194304 | tf_op jit(solution)/shard_map/two_phase_attention/pallas_call | solution.py:341
  55.6 1.0 %copy.11 = bf16[1024,4,128]{2,1,0:T(4,128)(2,1)} copy(bf16[1024,4,128]{2,1,0:T(4,128)(2,1)S(1)} %bitcast.4) | data formatting | bytes 2097152
  56.6 0.6 %copy.12 = bf16[8,128]{1,0:T(8,128)(2,1)} copy(bf16[8,128]{1,0:T(8,128)(2,1)S(1)} %get-tuple-element.9) | data formatting | bytes 4096

commit v5 on v4

--- a/solution.py
+++ b/solution.py
@@ -13,6 +13,7 @@
 HD, GROUP, BLOCK, QTOK = 128, 4, 1024, 64
 ROWS = BLOCK * GROUP
 COLS = 1024
+FAR_FIRST = sorted(range(1, N_Z), key=lambda d: abs(d - N_Z // 2))
 F32, BF16 = jnp.float32, jnp.bfloat16
 C2 = HD**-0.5 * math.log2(math.e)
 
@@ -52,7 +53,7 @@
     a_rank, a_z = 2 * (anchor // 32) + anchor % 2, (anchor // 2) % N_Z
     is_anchor = anchor == c
 
-    near = [(y, 1 - k), (1 - y, k), (1 - y, 1 - k)]
+    near = [(1 - y, k), (1 - y, 1 - k), (y, 1 - k)]
     barrier = pltpu.get_barrier_semaphore()
     for to_y, to_k in near:
         signal(barrier, ctx=ctx_at(to_y, z, to_k))
@@ -94,7 +95,7 @@
         cand[half][rank] = pairs_v[rank, half]
         arrived(cand[half].at[pl.ds(0, 3)], half)
         z_src[half] = cand[half][a_rank]
-        for d in range(1, N_Z):
+        for d in FAR_FIRST:
             to = (z + d) % N_Z
             send(z_src.at[half, to], z_cand[half].at[z], 2 + half, ctx=ctx_at(y, to, k))
         z_cand[half][z] = z_src[half, z]
@@ -102,7 +103,7 @@
     def z_gather(half):
         arrived(z_cand[half].at[pl.ds(0, N_Z - 1)], 2 + half)
         far[half][rank, z] = z_cand[half][a_z]
-        for d in range(1, N_Z):
+        for d in FAR_FIRST:
             to = (z + d) % N_Z
             send(far[half].at[rank, z], far[half].at[rank, z], 4 + half, ctx=ctx_at(y, to, k))
 
@@ -169,7 +170,7 @@
         return both, weight_sum, mixed
 
     def local_peers():
-        for d in range(1, 16):
+        for d in range(15, 0, -1):
             to_z, to_rank = (z_lo + d // 4) % 4, (rank + d) % 4
             yield 4 * to_z + to_rank, ctx_at(to_rank // 2, 4 * z_hi + to_z, to_rank % 2)
 
@@ -185,7 +186,7 @@
         arrived(q_all.at[pl.ds(0, 3)], 16)
         arrived(akv.at[pl.ds(0, 3)], 17)
         tokens = [pl.ds(2 * z, 2), pl.ds(2 * (N_Z + z), 2)]
-        for d in range(1, N_Z):
+        for d in FAR_FIRST:
             to = ctx_at(y, (z + d) % N_Z, k)
             for two in tokens:
                 send(q_all.at[two], q_all.at[two], 8, ctx=to)

time: 57.3 us -> 56.6 us (0.988)
  Pallas kernels: 54.4 us -> 53.7 us
    pallas_call x1, Pallas kernels: 54.4 us -> 53.7 us  [on_device(): pl.pallas_call(kernel, out_shape=(jax.ShapeDtypeStruct((ROWS, HD), BF16),...]
where the time goes in v5:
time: 56.6 us; the launch traced here: 56.5 us
  Pallas kernels  53.7 us (95%)
  local copies, waits for them, and re-layouts  1.55 us (3%)
  between operations  1.29 us (2%)
    pallas_call x1, Pallas kernels, on_device(): pl.pallas_call(kernel, out_shape=(jax.ShapeDtypeStruct((ROWS, HD), BF16),...  53.7 us
    unnamed x2, local copies, waits for them, and re-layouts  1.55 us

profile of v5, /device:TPU:1, one launch (start us, length us, event | category | flops | bytes accessed | tf_op | source)
XLA Modules:
  0.0 56.5 jit_solution(2334032748444962001)
XLA Ops:
  1.3 53.7 %two_phase_attention.1 = (bf16[4096,128]{1,0:T(8,128)(2,1)S(1)}, bf16[8,128]{1,0:T(8,128)(2,1)S(1)}) custom-call(s32[1]{0:T(128)S(6)} %copy.10.anchor_ref, bf16[4096,128]{1,0:T(8,128)(2,1)} %bitcast.5, bf16[4,2,16,16,128]{4,3,2,1,0:T(8,128)(2,1)} %bitcast.6, bf16[1,4,128]{2,1,0:T(4,128)(2,1)} %aq_hbm.1, bf16[1,2,128]{2,1,0:T(2,128)(2,1)} %bitcast.7, ...), custom_call_target="tpu_custom_call" | custom-call | flops 4294967296 | bytes 4194304 | tf_op jit(solution)/shard_map/two_phase_attention/pallas_call | solution.py:342
  55.0 1.0 %copy.11 = bf16[1024,4,128]{2,1,0:T(4,128)(2,1)} copy(bf16[1024,4,128]{2,1,0:T(4,128)(2,1)S(1)} %bitcast.4) | data formatting | bytes 2097152
  55.9 0.6 %copy.12 = bf16[8,128]{1,0:T(8,128)(2,1)} copy(bf16[8,128]{1,0:T(8,128)(2,1)S(1)} %get-tuple-element.9) | data formatting | bytes 4096
